TPU v7x, 32 devices: a whole 2x2x4 slice. The times are simulated.
32 devices in a mesh: scene: 2 (over x), tile: 8 (over z, y), date: 2 (over core).
Axes of the slice: x: 2, y: 2, z: 4, core: 2. Of those that a mesh axis runs over, the one named last changes fastest.
Arguments:
- slc_real: bfloat16 [32, 512, 256], P('date', ('scene', 'tile')), parts along dimension 1, may hold values from -4.5 to 4.5
- slc_imag: bfloat16 [32, 512, 256], P('date', ('scene', 'tile')), parts along dimension 1, may hold values from -4.5 to 4.5
- pair_offset: int32 [32, 4], replicated, may hold values from 1 to 5, as said below
- pair_weight: int32 [128, 512, 256], P(None, ('scene', 'tile', 'date')), parts along dimension 1, may hold values from 1 to 255
Outputs:
- increments: float32 [31, 512, 256], P(None, ('scene', 'tile', 'date')), parts along dimension 1
There are 2 independent parts, one for each index of `scene`. A program takes and returns all parts, laid end to end along the dimension named above; an argument that names none is the same for every part. Nothing has to cross between parts.
Inputs may be any that keep to these rules, and one draw needn't show every extreme that they name: `pair_offset`: each row holds 4 different offsets in increasing order; 1 and 5 are in every row.
All inputs are finite; a program needn't handle non-finite values.
Results may differ from a plain program's by a relative error of at most 0.0003.
Values may be sent and summed in bfloat16 or wider, within the bound.
A program may use at most 128 MiB of HBM per device.

v0:
```python
import jax
import jax.numpy as jnp
from jax import lax
from jax.sharding import PartitionSpec as P

K = 4
SPAN = 5
SWEEPS = 8
PASSES = 3
STEPS = 2


unwrap_damping = 0.08
column_weight = 0.15
solve_damping = 0.1
residual_scale = 0.3


def extended(block, sides, width):
    for axis, dim in sides:
        count = lax.axis_size(axis)
        forward = [(i, i + 1) for i in range(count - 1)]
        backward = [(target, source) for source, target in forward]
        low = lax.ppermute(
            lax.slice_in_dim(block, block.shape[dim] - width, None, axis=dim), axis, forward
        )
        high = lax.ppermute(lax.slice_in_dim(block, 0, width, axis=dim), axis, backward)
        block = jnp.concatenate([low, block, high], axis=dim)
    return block


def from_left(values):
    widths = [(0, 0)] * (values.ndim - 1) + [(1, 0)]
    return jnp.pad(values[..., :-1], widths)


def from_right(values):
    widths = [(0, 0)] * (values.ndim - 1) + [(0, 1)]
    return jnp.pad(values[..., 1:], widths)


def coupling(here_re, here_im, there_re, there_im, weight):
    magnitude = jnp.sqrt(
        (here_re * here_re + here_im * here_im) * (there_re * there_re + there_im * there_im)
    )
    link_value = weight * magnitude / (magnitude + 1.0)
    slope_value = (here_im * there_re - here_re * there_im) / (magnitude + 1.0)
    return (link_value, slope_value)


def box_mean(values):
    row_sum = values[..., :-2, :] + values[..., 1:-1, :] + values[..., 2:, :]
    return (from_left(row_sum) + row_sum + from_right(row_sum)) / 9.0


def cell_terms(smooth_re, smooth_im):
    centre_re = smooth_re[..., 1:-1, :]
    centre_im = smooth_im[..., 1:-1, :]
    link_up, slope_up = coupling(
        centre_re, centre_im, smooth_re[..., :-2, :], smooth_im[..., :-2, :], 1.0
    )
    link_down, slope_down = coupling(
        centre_re, centre_im, smooth_re[..., 2:, :], smooth_im[..., 2:, :], 1.0
    )
    link_left, slope_left = coupling(
        centre_re, centre_im, from_left(centre_re), from_left(centre_im), column_weight
    )
    link_right, slope_right = coupling(
        centre_re, centre_im, from_right(centre_re), from_right(centre_im), column_weight
    )
    denominator = link_up + link_down + link_left + link_right + unwrap_damping
    source = (
        link_up * slope_up
        + link_down * slope_down
        + link_left * slope_left
        + link_right * slope_right
    )
    return (link_up, link_down, link_left, link_right, denominator, source)


def relax_once(unwrapped, above, below, stencil):
    link_up, link_down, link_left, link_right, denominator, source = stencil
    summed = (
        source
        + link_up * above
        + link_down * below
        + link_left * from_left(unwrapped)
        + link_right * from_right(unwrapped)
    )
    return summed / denominator


def pair_tables(pair_offset):
    date_count = pair_offset.shape[0]
    per_date = pair_offset.shape[1]
    first_date = jnp.arange(date_count * per_date, dtype=jnp.int32) // per_date
    second = first_date + pair_offset.reshape(-1)
    validity = (second < date_count).astype(jnp.float32)
    unknown = jnp.arange(date_count - 1, dtype=jnp.int32)
    design = (
        (unknown[None, :] >= first_date[:, None]) & (unknown[None, :] < second[:, None])
    ).astype(jnp.float32)
    return (validity, design)


def forward(design, values):
    return jnp.dot(
        design, values, precision=lax.Precision.HIGHEST, preferred_element_type=jnp.float32
    )


def backward(design, values):
    return jnp.dot(
        design.T, values, precision=lax.Precision.HIGHEST, preferred_element_type=jnp.float32
    )


def invert(phases, base_weight, design):
    increments = jnp.zeros((design.shape[1], phases.shape[1]), jnp.float32)
    for pass_index in range(PASSES):
        scaled = (phases - forward(design, increments)) / residual_scale
        weights = base_weight / (1.0 + scaled * scaled)
        diagonal = backward(design, weights) + solve_damping
        for step_index in range(STEPS):
            gradient = (
                backward(design, weights * (phases - forward(design, increments)))
                - solve_damping * increments
            )
            increments = increments + 1.0 / SPAN * gradient / diagonal
    return increments


def interfere(source_stack, first_count, second_date, validity):
    height = source_stack.shape[2]
    columns = source_stack.shape[3]
    last_index = source_stack.shape[1] - 1
    picked = jnp.minimum(second_date, last_index)
    shape_out = (first_count, K, height, columns)
    first_re = (
        jnp.broadcast_to(source_stack[0, :first_count, None], shape_out)
        .reshape(first_count * K, height, columns)
        .astype(jnp.float32)
    )
    first_im = (
        jnp.broadcast_to(source_stack[1, :first_count, None], shape_out)
        .reshape(first_count * K, height, columns)
        .astype(jnp.float32)
    )
    second_re = jnp.take(source_stack[0], picked, axis=0).astype(jnp.float32)
    second_im = jnp.take(source_stack[1], picked, axis=0).astype(jnp.float32)
    pair_real = validity * (first_re * second_re + first_im * second_im)
    pair_imag = validity * (first_im * second_re - first_re * second_im)
    return jnp.stack([pair_real, pair_imag])


def unwrap(formed, first_row, shard_rows, image_rows, rim_depth, refresh):
    smooth_rows = formed.shape[2] - 2
    global_row = first_row - rim_depth + jnp.arange(smooth_rows, dtype=jnp.int32)
    inside = ((global_row >= 0) & (global_row < image_rows)).astype(jnp.float32)[:, None]
    smooth_re = box_mean(formed[0]) * inside
    smooth_im = box_mean(formed[1]) * inside
    stencil = cell_terms(smooth_re, smooth_im)
    pair_count = formed.shape[1]
    columns = formed.shape[3]
    unwrapped = jnp.zeros((pair_count, shard_rows + 2 * rim_depth, columns), jnp.float32)
    for sweep_index in range(SWEEPS):
        if sweep_index > 0 and sweep_index % rim_depth == 0:
            unwrapped = refresh(unwrapped[:, rim_depth : rim_depth + shard_rows])
        interior = relax_once(unwrapped[:, 1:-1], unwrapped[:, :-2], unwrapped[:, 2:], stencil)
        unwrapped = jnp.concatenate([unwrapped[:, :1], interior, unwrapped[:, -1:]], axis=1)
    return unwrapped[:, rim_depth : rim_depth + shard_rows]


def local(slc_real, slc_imag, pair_offset, pair_weight):
    tile_rows = slc_real.shape[1]
    columns = slc_real.shape[2]
    date_count = pair_offset.shape[0]
    date_group = lax.axis_index("date")
    tile_index = lax.axis_index("tile")
    group_count = lax.axis_size("date")
    image_rows = tile_rows * lax.axis_size("tile")
    rim_depth = 1
    images = jnp.stack([slc_real, slc_imag])
    validity, design = pair_tables(pair_offset)
    row_blocks = lax.all_to_all(images, "date", split_axis=2, concat_axis=1, tiled=True)
    shard_rows = row_blocks.shape[2]
    first_row = (tile_index * group_count + date_group) * shard_rows
    second_date = (jnp.arange(date_count, dtype=jnp.int32)[:, None] + pair_offset).reshape(-1)
    pair_maps = interfere(row_blocks, date_count, second_date, validity[:, None, None])
    formed = extended(pair_maps, ((("tile", "date"), 2),), rim_depth + 1)

    def refresh(values):
        return extended(values, ((("tile", "date"), 1),), rim_depth)

    phases = unwrap(formed, first_row, shard_rows, image_rows, rim_depth, refresh)
    base_weight = pair_weight.astype(jnp.float32) / 255.0 * validity[:, None, None]
    pair_count = phases.shape[0]
    local_rows = phases.shape[1]
    increments = invert(phases.reshape(pair_count, -1), base_weight.reshape(pair_count, -1), design)
    return increments.reshape(design.shape[1], local_rows, columns)


def solution(mesh):
    placed = (
        P("date", ("scene", "tile"), None),
        P("date", ("scene", "tile"), None),
        P(),
        P(None, ("scene", "tile", "date"), None),
    )
    return jax.shard_map(
        local,
        mesh=mesh,
        in_specs=placed,
        out_specs=P(None, ("scene", "tile", "date"), None),
        check_vma=False,
    )
```

profile of v0, /device:TPU:13, one launch (start us, length us, event | category | flops | bytes accessed | tf_op | source)
XLA Modules:
  0.0 168.6 jit_solution(14839721943044974520)
XLA Ops:
  2.2 4.2 %all-to-all-start = ((bf16[2,16,32,256]{3,1,0,2:T(8,128)(2,1)}), bf16[2,16,32,256]{3,1,0,2:T(8,128)(2,1)S(1)}, u32[]{:S(2)}, u32[]{:S(2)}) async-start(bf16[2,16,32,256]{3,1,0,2:T(8,128)(2,1)} %pad_maximum_fusion.17), calls=%async_computation | async-start | bytes 1048576 | tf_op jit(solution)/shard_map/all_to_all | solution.py:185
  16.4 3.4 %collective-permute-start = (f32[2,128,2,256]{3,2,1,0:T(2,128)}, f32[2,128,2,256]{3,2,1,0:T(2,128)S(1)}, u32[]{:S(2)}, u32[]{:S(2)}) collective-permute-start(f32[2,128,2,256]{3,2,1,0:T(2,128)} %get-tuple-element.14), channel_id=1, source_target_pairs={{0,1},{1,2},{2,3},{3,4},{4,5},{5,6},{6,7},{7,8},{8,9},{9,10},{10,1... | collective-permute-start | bytes 1572872 | tf_op jit(solution)/shard_map/ppermute | solution.py:24
  23.8 2.9 %copy.20 = f32[16,8,16,256]{3,1,2,0:T(8,128)} copy(f32[16,8,16,256]{3,2,1,0:T(8,128)S(1)} %bitcast.63) | data formatting | bytes 4194304
  26.8 4.7 %collective-permute-done.1 = f32[2,128,2,256]{3,2,1,0:T(2,128)} collective-permute-done((f32[2,128,2,256]{3,2,1,0:T(2,128)S(1)}, f32[2,128,2,256]{3,2,1,0:T(2,128)}, u32[]{:S(2)}, u32[]{:S(2)}) %collective-permute-start.1) | collective-permute-done | bytes 524320 | tf_op jit(solution)/shard_map/ppermute | solution.py:27
  31.5 2.6 %pad_maximum_fusion = f32[2,128,20,256]{3,2,1,0:T(8,128)S(1)} fusion(f32[2,128,2,256]{3,2,1,0:T(2,128)} %collective-permute-done.1, f32[1,128,16,256]{3,2,1,0:T(8,128)} %bitcast.59, f32[1,128,16,256]{3,2,1,0:T(8,128)S(1)} %bitcast.57, f32[2,128,2,256]{3,2,1,0:T(2,128)S(1)} %collective-permute-done), kind=kLoop, calls=%fused_computation.2 | loop fusion | flops 3932160 | bytes 10485760 | tf_op jit(solution)/shard_map/concatenate | solution.py:28
  35.1 2.7 %fusion.103 = (f32[128,18,255]{2,1,0:T(8,128)S(1)}, f32[128,18,255]{2,1,0:T(8,128)}) fusion(f32[128,18,256]{2,1,0:T(8,128)S(1)} %slice_add_fusion.2), kind=kLoop, calls=%fused_computation.169 | loop fusion | bytes 9400320 | tf_op jit(solution)/shard_map/slice | solution.py:34
  38.5 3.8 %fusion.104 = (f32[128,18,255]{2,1,0:T(8,128)}, f32[128,18,255]{2,1,0:T(8,128)}) fusion(f32[128,18,256]{2,1,0:T(8,128)S(1)} %slice_add_fusion), kind=kLoop, calls=%fused_computation.170 | loop fusion | bytes 9400320 | tf_op jit(solution)/shard_map/slice | solution.py:34
  42.2 5.3 %add_multiply_fusion.1 = (f32[128,18,256]{2,1,0:T(8,128)S(1)}, f32[128,18,256]{2,1,0:T(8,128)S(1)}) fusion(f32[128,18,255]{2,1,0:T(8,128)} %get-tuple-element.23, f32[128,18,255]{2,1,0:T(8,128)S(1)} %get-tuple-element.22, f32[18]{0:T(128)S(1)} %and_select_fusion, f32[128,18,255]{2,1,0:T(8,128)} %get-tuple-element.25, f32[128,18,255]{2,1,0:T(8,128)} %get-tuple-element.24, ...), kind=kLoop, calls=%fused_computation.48 | loop fusion | flops 5898240 | bytes 28274760 | tf_op jit(solution)/shard_map/mul | solution.py:160
  49.7 2.9 %fusion.102 = (f32[128,16,255]{2,1,0:T(8,128)}, f32[128,16,255]{2,1,0:T(8,128)}) fusion(f32[128,18,256]{2,1,0:T(8,128)S(1)} %get-tuple-element.57), kind=kLoop, calls=%fused_computation.168 | loop fusion | bytes 8355840 | tf_op jit(solution)/shard_map/slice | solution.py:34
  52.8 9.2 %fusion.80 = (f32[128,16,256]{2,1,0:T(8,128)S(1)}, f32[128,16,256]{2,1,0:T(8,128)S(1)}, f32[128,16,256]{2,1,0:T(8,128)S(1)}, f32[128,16,256]{2,1,0:T(8,128)S(1)}...) fusion(f32[128,16,255]{2,1,0:T(8,128)S(1)} %broadcast.202, f32[128,16,255]{2,1,0:T(8,128)} %get-tuple-element.21, ...), kind=kLoop, calls=%fused_computation.132 | loop fusion | flops 34078720 | bytes 35610624 | tf_op jit(solution)/shard_map/div | solution.py:90
  64.1 4.1 %collective-permute-start.3 = (f32[128,1,256]{2,1,0:T(1,128)S(1)}, f32[128,1,256]{2,1,0:T(1,128)S(1)}, u32[]{:S(2)}, u32[]{:S(2)}) collective-permute-start(f32[128,1,256]{2,1,0:T(1,128)S(1)} %get-tuple-element.53), channel_id=1, source_target_pairs={{1,0},{2,1},{3,2},{4,3},{5,4},{6,5},{7,6},{8,7},{9,8},{10,9},{11,1... | collective-permute-start | bytes 393224 | tf_op jit(solution)/shard_map/ppermute | solution.py:27
  68.9 3.4 %collective-permute-done.3 = f32[128,1,256]{2,1,0:T(1,128)S(1)} collective-permute-done((f32[128,1,256]{2,1,0:T(1,128)S(1)}, f32[128,1,256]{2,1,0:T(1,128)S(1)}, u32[]{:S(2)}, u32[]{:S(2)}) %collective-permute-start.3) | collective-permute-done | bytes 131104 | tf_op jit(solution)/shard_map/ppermute | solution.py:27
  72.3 2.7 %fusion.74 = f32[128,16,256]{2,1,0:T(8,128)S(1)} fusion(f32[128,16,256]{2,1,0:T(8,128)S(1)} %get-tuple-element.11, f32[128,1,256]{2,1,0:T(1,128)S(1)} %collective-permute-done.3, f32[128,16,256]{2,1,0:T(8,128)S(1)} %get-tuple-element.6, f32[128,16,256]{2,1,0:T(8,128)S(1)} %get-tuple-element.7, f32[128,16,256]{2,1,0:T(8,128)S(1)} %get-tuple-element.8, ...), kind=kLoop, calls=%fused_computation.121 | loop fusion | flops 7864320 | bytes 19120128 | tf_op jit(solution)/shard_map/div | solution.py:90
  80.3 4.0 %collective-permute-done.5 = f32[128,1,256]{2,1,0:T(1,128)S(1)} collective-permute-done((f32[128,1,256]{2,1,0:T(1,128)S(1)}, f32[128,1,256]{2,1,0:T(1,128)S(1)}, u32[]{:S(2)}, u32[]{:S(2)}) %collective-permute-start.5) | collective-permute-done | bytes 131104 | tf_op jit(solution)/shard_map/ppermute | solution.py:27
  84.3 2.6 %fusion.67 = f32[128,16,256]{2,1,0:T(8,128)S(1)} fusion(f32[128,16,256]{2,1,0:T(8,128)S(1)} %get-tuple-element.11, f32[128,1,256]{2,1,0:T(1,128)S(1)} %collective-permute-done.5, f32[128,16,256]{2,1,0:T(8,128)S(1)} %fusion.74, f32[128,16,256]{2,1,0:T(8,128)S(1)} %get-tuple-element.7, f32[128,16,256]{2,1,0:T(8,128)S(1)} %get-tuple-element.8, ...), kind=kLoop, calls=%fused_computation.112 | loop fusion | flops 7864320 | bytes 19120128 | tf_op jit(solution)/shard_map/div | solution.py:90
  92.2 4.0 %collective-permute-done.7 = f32[128,1,256]{2,1,0:T(1,128)S(1)} collective-permute-done((f32[128,1,256]{2,1,0:T(1,128)S(1)}, f32[128,1,256]{2,1,0:T(1,128)S(1)}, u32[]{:S(2)}, u32[]{:S(2)}) %collective-permute-start.7) | collective-permute-done | bytes 131104 | tf_op jit(solution)/shard_map/ppermute | solution.py:27
  96.2 2.6 %fusion.60 = f32[128,16,256]{2,1,0:T(8,128)S(1)} fusion(f32[128,16,256]{2,1,0:T(8,128)S(1)} %get-tuple-element.11, f32[128,1,256]{2,1,0:T(1,128)S(1)} %collective-permute-done.7, f32[128,16,256]{2,1,0:T(8,128)S(1)} %fusion.67, f32[128,16,256]{2,1,0:T(8,128)S(1)} %get-tuple-element.7, f32[128,16,256]{2,1,0:T(8,128)S(1)} %get-tuple-element.8, ...), kind=kLoop, calls=%fused_computation.103 | loop fusion | flops 7864320 | bytes 19120128 | tf_op jit(solution)/shard_map/div | solution.py:90
  104.2 4.0 %collective-permute-done.9 = f32[128,1,256]{2,1,0:T(1,128)S(1)} collective-permute-done((f32[128,1,256]{2,1,0:T(1,128)S(1)}, f32[128,1,256]{2,1,0:T(1,128)S(1)}, u32[]{:S(2)}, u32[]{:S(2)}) %collective-permute-start.9) | collective-permute-done | bytes 131104 | tf_op jit(solution)/shard_map/ppermute | solution.py:27
  108.2 2.6 %fusion.53 = f32[128,16,256]{2,1,0:T(8,128)S(1)} fusion(f32[128,16,256]{2,1,0:T(8,128)S(1)} %get-tuple-element.11, f32[128,1,256]{2,1,0:T(1,128)S(1)} %collective-permute-done.9, f32[128,16,256]{2,1,0:T(8,128)S(1)} %fusion.60, f32[128,16,256]{2,1,0:T(8,128)S(1)} %get-tuple-element.7, f32[128,16,256]{2,1,0:T(8,128)S(1)} %get-tuple-element.8, ...), kind=kLoop, calls=%fused_computation.94 | loop fusion | flops 7864320 | bytes 19120128 | tf_op jit(solution)/shard_map/div | solution.py:90
  116.1 4.0 %collective-permute-done.11 = f32[128,1,256]{2,1,0:T(1,128)S(1)} collective-permute-done((f32[128,1,256]{2,1,0:T(1,128)S(1)}, f32[128,1,256]{2,1,0:T(1,128)S(1)}, u32[]{:S(2)}, u32[]{:S(2)}) %collective-permute-start.11) | collective-permute-done | bytes 131104 | tf_op jit(solution)/shard_map/ppermute | solution.py:27
  120.1 2.6 %fusion.46 = f32[128,16,256]{2,1,0:T(8,128)S(1)} fusion(f32[128,16,256]{2,1,0:T(8,128)S(1)} %get-tuple-element.11, f32[128,1,256]{2,1,0:T(1,128)S(1)} %collective-permute-done.11, f32[128,16,256]{2,1,0:T(8,128)S(1)} %fusion.53, f32[128,16,256]{2,1,0:T(8,128)S(1)} %get-tuple-element.7, f32[128,16,256]{2,1,0:T(8,128)S(1)} %get-tuple-element.8, ...), kind=kLoop, calls=%fused_computation.85 | loop fusion | flops 7864320 | bytes 19120128 | tf_op jit(solution)/shard_map/div | solution.py:90
  128.0 4.0 %collective-permute-done.13 = f32[128,1,256]{2,1,0:T(1,128)S(1)} collective-permute-done((f32[128,1,256]{2,1,0:T(1,128)S(1)}, f32[128,1,256]{2,1,0:T(1,128)S(1)}, u32[]{:S(2)}, u32[]{:S(2)}) %collective-permute-start.13) | collective-permute-done | bytes 131104 | tf_op jit(solution)/shard_map/ppermute | solution.py:27
  140.0 4.0 %collective-permute-done.15 = f32[128,1,256]{2,1,0:T(1,128)S(1)} collective-permute-done((f32[128,1,256]{2,1,0:T(1,128)S(1)}, f32[128,1,256]{2,1,0:T(1,128)S(1)}, u32[]{:S(2)}, u32[]{:S(2)}) %collective-permute-start.15) | collective-permute-done | bytes 131104 | tf_op jit(solution)/shard_map/ppermute | solution.py:27
  144.0 2.8 %fusion.32 = f32[128,16,256]{2,1,0:T(8,128)S(1)} fusion(f32[128,16,256]{2,1,0:T(8,128)S(1)} %get-tuple-element.11, f32[128,1,256]{2,1,0:T(1,128)S(1)} %collective-permute-done.15, f32[128,16,256]{2,1,0:T(8,128)S(1)} %fusion.39, f32[128,16,256]{2,1,0:T(8,128)S(1)} %get-tuple-element.7, f32[128,16,256]{2,1,0:T(8,128)S(1)} %get-tuple-element.8, ...), kind=kLoop, calls=%fused_computation.67 | loop fusion | flops 7864320 | bytes 19120128 | tf_op jit(solution)/shard_map/div | solution.py:90
  (91 shorter events, 78.9 us)
Async XLA Ops:
  0.0 6.3 %copy-start.2 = (s32[32,4]{0,1:T(4,128)S(1)}, s32[32,4]{0,1:T(4,128)}, u32[]{:S(2)}) copy-start(s32[32,4]{0,1:T(4,128)} %param.8) | copy-start | bytes 1540
  2.2 5.5 %all-to-all-start = ((bf16[2,16,32,256]{3,1,0,2:T(8,128)(2,1)}), bf16[2,16,32,256]{3,1,0,2:T(8,128)(2,1)S(1)}, u32[]{:S(2)}, u32[]{:S(2)}) async-start(bf16[2,16,32,256]{3,1,0,2:T(8,128)(2,1)} %pad_maximum_fusion.17), calls=%async_computation | async-start | bytes 1048576 | tf_op jit(solution)/shard_map/all_to_all | solution.py:185
  15.0 1.5 copy-start
  16.4 10.3 %collective-permute-start = (f32[2,128,2,256]{3,2,1,0:T(2,128)}, f32[2,128,2,256]{3,2,1,0:T(2,128)S(1)}, u32[]{:S(2)}, u32[]{:S(2)}) collective-permute-start(f32[2,128,2,256]{3,2,1,0:T(2,128)} %get-tuple-element.14), channel_id=1, source_target_pairs={{0,1},{1,2},{2,3},{3,4},{4,5},{5,6},{6,7},{7,8},{8,9},{9,10},{10,1... | collective-permute-start | bytes 1572872 | tf_op jit(solution)/shard_map/ppermute | solution.py:24
  19.9 11.6 %collective-permute-start.1 = (f32[2,128,2,256]{3,2,1,0:T(2,128)S(1)}, f32[2,128,2,256]{3,2,1,0:T(2,128)}, u32[]{:S(2)}, u32[]{:S(2)}) collective-permute-start(f32[2,128,2,256]{3,2,1,0:T(2,128)S(1)} %get-tuple-element.15), channel_id=1, source_target_pairs={{1,0},{2,1},{3,2},{4,3},{5,4},{6,5},{7,6},{8,7},{9,8},{10,9},{11,1... | collective-permute-start | bytes 1572872 | tf_op jit(solution)/shard_map/ppermute | solution.py:27
  62.2 6.7 %collective-permute-start.2 = (f32[128,1,256]{2,1,0:T(1,128)S(1)}, f32[128,1,256]{2,1,0:T(1,128)S(1)}, u32[]{:S(2)}, u32[]{:S(2)}) collective-permute-start(f32[128,1,256]{2,1,0:T(1,128)S(1)} %get-tuple-element.52), channel_id=1, source_target_pairs={{0,1},{1,2},{2,3},{3,4},{4,5},{5,6},{6,7},{7,8},{8,9},{9,10},{10,1... | collective-permute-start | bytes 393224 | tf_op jit(solution)/shard_map/ppermute | solution.py:24
  64.1 8.2 %collective-permute-start.3 = (f32[128,1,256]{2,1,0:T(1,128)S(1)}, f32[128,1,256]{2,1,0:T(1,128)S(1)}, u32[]{:S(2)}, u32[]{:S(2)}) collective-permute-start(f32[128,1,256]{2,1,0:T(1,128)S(1)} %get-tuple-element.53), channel_id=1, source_target_pairs={{1,0},{2,1},{3,2},{4,3},{5,4},{6,5},{7,6},{8,7},{9,8},{10,9},{11,1... | collective-permute-start | bytes 393224 | tf_op jit(solution)/shard_map/ppermute | solution.py:27
  75.2 5.1 %collective-permute-start.4 = (f32[128,1,256]{2,1,0:T(1,128)S(1)}, f32[128,1,256]{2,1,0:T(1,128)S(1)}, u32[]{:S(2)}, u32[]{:S(2)}) collective-permute-start(f32[128,1,256]{2,1,0:T(1,128)S(1)} %get-tuple-element.48), channel_id=1, source_target_pairs={{0,1},{1,2},{2,3},{3,4},{4,5},{5,6},{6,7},{7,8},{8,9},{9,10},{10,1... | collective-permute-start | bytes 393224 | tf_op jit(solution)/shard_map/ppermute | solution.py:24
  77.1 7.2 %collective-permute-start.5 = (f32[128,1,256]{2,1,0:T(1,128)S(1)}, f32[128,1,256]{2,1,0:T(1,128)S(1)}, u32[]{:S(2)}, u32[]{:S(2)}) collective-permute-start(f32[128,1,256]{2,1,0:T(1,128)S(1)} %get-tuple-element.49), channel_id=1, source_target_pairs={{1,0},{2,1},{3,2},{4,3},{5,4},{6,5},{7,6},{8,7},{9,8},{10,9},{11,1... | collective-permute-start | bytes 393224 | tf_op jit(solution)/shard_map/ppermute | solution.py:27
  87.1 5.1 %collective-permute-start.6 = (f32[128,1,256]{2,1,0:T(1,128)S(1)}, f32[128,1,256]{2,1,0:T(1,128)S(1)}, u32[]{:S(2)}, u32[]{:S(2)}) collective-permute-start(f32[128,1,256]{2,1,0:T(1,128)S(1)} %get-tuple-element.44), channel_id=1, source_target_pairs={{0,1},{1,2},{2,3},{3,4},{4,5},{5,6},{6,7},{7,8},{8,9},{9,10},{10,1... | collective-permute-start | bytes 393224 | tf_op jit(solution)/shard_map/ppermute | solution.py:24
  89.0 7.2 %collective-permute-start.7 = (f32[128,1,256]{2,1,0:T(1,128)S(1)}, f32[128,1,256]{2,1,0:T(1,128)S(1)}, u32[]{:S(2)}, u32[]{:S(2)}) collective-permute-start(f32[128,1,256]{2,1,0:T(1,128)S(1)} %get-tuple-element.45), channel_id=1, source_target_pairs={{1,0},{2,1},{3,2},{4,3},{5,4},{6,5},{7,6},{8,7},{9,8},{10,9},{11,1... | collective-permute-start | bytes 393224 | tf_op jit(solution)/shard_map/ppermute | solution.py:27
  99.0 5.1 %collective-permute-start.8 = (f32[128,1,256]{2,1,0:T(1,128)S(1)}, f32[128,1,256]{2,1,0:T(1,128)S(1)}, u32[]{:S(2)}, u32[]{:S(2)}) collective-permute-start(f32[128,1,256]{2,1,0:T(1,128)S(1)} %get-tuple-element.40), channel_id=1, source_target_pairs={{0,1},{1,2},{2,3},{3,4},{4,5},{5,6},{6,7},{7,8},{8,9},{9,10},{10,1... | collective-permute-start | bytes 393224 | tf_op jit(solution)/shard_map/ppermute | solution.py:24
  101.0 7.2 %collective-permute-start.9 = (f32[128,1,256]{2,1,0:T(1,128)S(1)}, f32[128,1,256]{2,1,0:T(1,128)S(1)}, u32[]{:S(2)}, u32[]{:S(2)}) collective-permute-start(f32[128,1,256]{2,1,0:T(1,128)S(1)} %get-tuple-element.41), channel_id=1, source_target_pairs={{1,0},{2,1},{3,2},{4,3},{5,4},{6,5},{7,6},{8,7},{9,8},{10,9},{11,1... | collective-permute-start | bytes 393224 | tf_op jit(solution)/shard_map/ppermute | solution.py:27
  111.0 5.1 %collective-permute-start.10 = (f32[128,1,256]{2,1,0:T(1,128)S(1)}, f32[128,1,256]{2,1,0:T(1,128)S(1)}, u32[]{:S(2)}, u32[]{:S(2)}) collective-permute-start(f32[128,1,256]{2,1,0:T(1,128)S(1)} %get-tuple-element.36), channel_id=1, source_target_pairs={{0,1},{1,2},{2,3},{3,4},{4,5},{5,6},{6,7},{7,8},{8,9},{9,10},{10,1... | collective-permute-start | bytes 393224 | tf_op jit(solution)/shard_map/ppermute | solution.py:24
  112.9 7.2 %collective-permute-start.11 = (f32[128,1,256]{2,1,0:T(1,128)S(1)}, f32[128,1,256]{2,1,0:T(1,128)S(1)}, u32[]{:S(2)}, u32[]{:S(2)}) collective-permute-start(f32[128,1,256]{2,1,0:T(1,128)S(1)} %get-tuple-element.37), channel_id=1, source_target_pairs={{1,0},{2,1},{3,2},{4,3},{5,4},{6,5},{7,6},{8,7},{9,8},{10,9},{11,1... | collective-permute-start | bytes 393224 | tf_op jit(solution)/shard_map/ppermute | solution.py:27
  122.9 5.1 %collective-permute-start.12 = (f32[128,1,256]{2,1,0:T(1,128)S(1)}, f32[128,1,256]{2,1,0:T(1,128)S(1)}, u32[]{:S(2)}, u32[]{:S(2)}) collective-permute-start(f32[128,1,256]{2,1,0:T(1,128)S(1)} %get-tuple-element.32), channel_id=1, source_target_pairs={{0,1},{1,2},{2,3},{3,4},{4,5},{5,6},{6,7},{7,8},{8,9},{9,10},{10,1... | collective-permute-start | bytes 393224 | tf_op jit(solution)/shard_map/ppermute | solution.py:24
  124.8 7.2 %collective-permute-start.13 = (f32[128,1,256]{2,1,0:T(1,128)S(1)}, f32[128,1,256]{2,1,0:T(1,128)S(1)}, u32[]{:S(2)}, u32[]{:S(2)}) collective-permute-start(f32[128,1,256]{2,1,0:T(1,128)S(1)} %get-tuple-element.33), channel_id=1, source_target_pairs={{1,0},{2,1},{3,2},{4,3},{5,4},{6,5},{7,6},{8,7},{9,8},{10,9},{11,1... | collective-permute-start | bytes 393224 | tf_op jit(solution)/shard_map/ppermute | solution.py:27
  134.8 5.1 %collective-permute-start.14 = (f32[128,1,256]{2,1,0:T(1,128)S(1)}, f32[128,1,256]{2,1,0:T(1,128)S(1)}, u32[]{:S(2)}, u32[]{:S(2)}) collective-permute-start(f32[128,1,256]{2,1,0:T(1,128)S(1)} %get-tuple-element.28), channel_id=1, source_target_pairs={{0,1},{1,2},{2,3},{3,4},{4,5},{5,6},{6,7},{7,8},{8,9},{9,10},{10,1... | collective-permute-start | bytes 393224 | tf_op jit(solution)/shard_map/ppermute | solution.py:24
  136.8 7.2 %collective-permute-start.15 = (f32[128,1,256]{2,1,0:T(1,128)S(1)}, f32[128,1,256]{2,1,0:T(1,128)S(1)}, u32[]{:S(2)}, u32[]{:S(2)}) collective-permute-start(f32[128,1,256]{2,1,0:T(1,128)S(1)} %get-tuple-element.29), channel_id=1, source_target_pairs={{1,0},{2,1},{3,2},{4,3},{5,4},{6,5},{7,6},{8,7},{9,8},{10,9},{11,1... | collective-permute-start | bytes 393224 | tf_op jit(solution)/shard_map/ppermute | solution.py:27
  148.4 1.6 copy-start.1
where the time goes:
time: 172 us; the launch traced here: 169 us
  other arithmetic  45.2 us (26%)
  starting transfers between devices  41.6 us (24%)
  waiting for transfers between devices  33.3 us (19%)
  local copies, waits for them, and re-layouts  29.7 us (17%)
  matrix products  18 us (10%)
    ppermute x8, waiting for transfers between devices, extended(): lax.ppermute(lax.slice_in_dim(block, 0, width, axis=dim), axis, backward)  32 us
    div x8, other arithmetic, relax_once(): return summed / denominator  27.7 us
    ppermute x8, starting transfers between devices, extended(): lax.ppermute(lax.slice_in_dim(block, 0, width, axis=dim), axis, backward)  20.6 us
    slice x11, local copies, waits for them, and re-layouts, from_left(): return jnp.pad(values[..., :-1], widths)  16.9 us
    ppermute x8, starting transfers between devices, extended(): lax.ppermute(lax.slice_in_dim(block, block.shape[dim] - width, None, axis...  16.8 us
    dot_general x9, matrix products, backward(): jnp.dot(design.T, values, precision=lax.Precision.HIGHEST, preferred_elem...  10.8 us
    dot_general x6, matrix products, forward(): jnp.dot(design, values, precision=lax.Precision.HIGHEST, preferred_elemen...  7.2 us
    unnamed x10, local copies, waits for them, and re-layouts  5.75 us
  transfers between devices with their start and end apart: 17, of which 9 were waited for; matrix products, arithmetic and copies ran while one was open for 6% of the time, Pallas kernels for 0%

commit v1 on v0

v1 whole, which is shorter than its diff:
```python
import functools

import jax
import jax.numpy as jnp
from jax import lax
from jax.experimental import pallas as pl
from jax.experimental.pallas import tpu as pltpu
from jax.sharding import PartitionSpec as P

SPAN = 5
SWEEPS = 8
PASSES = 3
STEPS = 2

unwrap_damping = 0.08
column_weight = 0.15
solve_damping = 0.1
residual_scale = 0.3

RIM = SWEEPS + 1
MESH = pl.DeviceIdType.MESH
F32 = jnp.float32
BF16 = jnp.bfloat16


def iota(shape, dim):
    return lax.broadcasted_iota(jnp.int32, shape, dim)


def one_hot(condition):
    return jnp.where(condition, 1.0, 0.0).astype(BF16)


def mm(a, b):
    return jnp.dot(a, b, preferred_element_type=F32)


def rcp(x):
    r = pl.reciprocal(x, approx=True)
    return r * (2.0 - x * r)


def split(x):
    high = x.astype(BF16)
    return high, (x - high.astype(F32)).astype(BF16)


def evens_first(columns):
    half = columns // 2
    new = iota((columns, columns), 1)
    old = jnp.where(new < half, 2 * new, 2 * (new - half) + 1)
    return one_hot(iota((columns, columns), 0) == old)


def exchange_kernel(tiles, re_ref, im_ref, out_ref, send_ref, send_sem, recv_sem):
    dates, tile_rows, columns = re_ref.shape
    shard = tile_rows // 2
    scene = lax.axis_index("scene")
    tile = lax.axis_index("tile")
    date = lax.axis_index("date")
    other = 1 - date
    has_up = tile > 0
    has_down = tile < tiles - 1
    barrier = pltpu.get_barrier_semaphore()

    def signal(to_tile, to_date):
        pl.semaphore_signal(
            barrier, inc=1, device_id=(scene, to_tile, to_date), device_id_type=MESH
        )

    signal(tile, other)

    @pl.when(jnp.logical_and(has_up, date == 0))
    def _():
        signal(tile - 1, 0)
        signal(tile - 1, 1)

    @pl.when(jnp.logical_and(has_down, date == 1))
    def _():
        signal(tile + 1, 0)
        signal(tile + 1, 1)

    order = evens_first(columns)
    count = dates * tile_rows
    new = iota((count, 1), 0)
    old = (new % dates) * tile_rows + new // dates
    rows_first = one_hot(iota((count, count), 1) == old)
    for part, ref in enumerate((re_ref, im_ref)):
        flat = ref[...].reshape(count, columns)
        moved = mm(rows_first, mm(flat, order).astype(BF16)).astype(BF16)
        send_ref[:, :, part * columns : (part + 1) * columns] = moved.reshape(
            tile_rows, dates, columns
        )

    pl.semaphore_wait(barrier, 1 + has_up.astype(jnp.int32) + has_down.astype(jnp.int32))

    span = shard + RIM
    mine = pl.ds(pl.multiple_of(date * dates, dates), dates)
    theirs = pl.ds(pl.multiple_of(other * dates, dates), dates)

    def copy(source, target, to_tile, to_date, send_at, recv_at):
        return pltpu.make_async_remote_copy(
            src_ref=send_ref.at[source],
            dst_ref=out_ref.at[target, mine],
            send_sem=send_sem.at[send_at],
            recv_sem=recv_sem.at[recv_at],
            device_id=(scene, to_tile, to_date),
            device_id_type=MESH,
        )

    up_copy = copy(pl.ds(0, RIM), pl.ds(span, RIM), tile - 1, 1, 0, 1 + date)
    down_copy = copy(
        pl.ds(tile_rows - RIM, RIM), pl.ds(0, RIM), tile + 1, 0, 1, 1 + date
    )
    across = copy(
        pl.ds(other * (tile_rows - span), span),
        pl.ds(date * RIM, span),
        tile,
        other,
        2,
        0,
    )

    @pl.when(has_up)
    def _():
        up_copy.start()

    @pl.when(has_down)
    def _():
        down_copy.start()

    across.start()

    out_ref[pl.ds((1 - date) * RIM, span), mine] = send_ref[
        pl.ds(date * (tile_rows - span), span)
    ]
    beyond = date * span
    missing = jnp.logical_or(
        jnp.logical_and(date == 0, tile == 0),
        jnp.logical_and(date == 1, tile == tiles - 1),
    )

    @pl.when(missing)
    def _():
        out_ref[pl.ds(beyond, RIM)] = jnp.zeros((RIM, 2 * dates, 2 * columns), BF16)

    across.wait_send()

    @pl.when(has_up)
    def _():
        up_copy.wait_send()

    @pl.when(has_down)
    def _():
        down_copy.wait_send()

    across.wait_recv()

    @pl.when(jnp.logical_not(missing))
    def _():
        for sender in range(2):
            pltpu.make_async_remote_copy(
                src_ref=send_ref.at[pl.ds(0, RIM)],
                dst_ref=out_ref.at[pl.ds(0, RIM), mine],
                send_sem=send_sem.at[0],
                recv_sem=recv_sem.at[1 + sender],
                device_id=(scene, tile, other),
                device_id_type=MESH,
            ).wait_recv()


def exchange(slc_real, slc_imag, tiles):
    dates, tile_rows, columns = slc_real.shape
    shape = (tile_rows // 2 + 2 * RIM, 2 * dates, 2 * columns)
    whole = pl.BlockSpec(memory_space=pltpu.VMEM)
    return pl.pallas_call(
        functools.partial(exchange_kernel, tiles),
        out_shape=jax.ShapeDtypeStruct(shape, BF16),
        in_specs=[whole, whole],
        out_specs=whole,
        scratch_shapes=[
            pltpu.VMEM((tile_rows, dates, 2 * columns), BF16),
            pltpu.SemaphoreType.DMA((3,)),
            pltpu.SemaphoreType.DMA((3,)),
        ],
        compiler_params=pltpu.CompilerParams(
            collective_id=0, has_side_effects=True, vmem_limit_bytes=24 << 20
        ),
    )(slc_real, slc_imag)


def unwrap_block(block, pairs, formed, coefs, phases, top, bottom, half):
    lines = formed.shape[0]
    here = pl.ds(pl.multiple_of(block * pairs, pairs), pairs)
    lane = iota((pairs, half), 1)
    not_first = jnp.where(lane > 0, 1.0, 0.0)
    not_last = jnp.where(lane < half - 1, 1.0, 0.0)
    between = not_first * column_weight
    back = lambda x: pltpu.roll(x, 1, 1)
    ahead = lambda x: pltpu.roll(x, half - 1, 1)

    def line(at):
        return [formed[at, here, part * half : (part + 1) * half] for part in range(4)]

    smooth = {}
    upper = {}
    levels = [dict() for _ in range(SWEEPS + 1)]

    def smooth_line(at, rows):
        result = []
        for part in (0, 2):
            even, odd = [rows[0][j] + rows[1][j] + rows[2][j] for j in (part, part + 1)]
            both = even + odd
            left = both + back(odd) * not_first
            right = both + ahead(even) * not_last
            if at == RIM - 1:
                left, right = left * top, right * top
            if at == lines - RIM:
                left, right = left * bottom, right * bottom
            result += [left, right]
        re_e, re_o, im_e, im_o = result
        size = []
        for re, im in ((re_e, im_e), (re_o, im_o)):
            power = re * re + im * im
            size.append(power * lax.rsqrt(jnp.maximum(power, 1e-30)))
        return (re_e, im_e, size[0]), (re_o, im_o, size[1])

    def couple(here_z, there_z, weight):
        product = here_z[2] * there_z[2]
        r = rcp(product + 81.0)
        link = product * r
        if weight is not None:
            link = link * weight
        cross = here_z[1] * there_z[0] - here_z[0] * there_z[1]
        return link, link * r * cross

    def stencil(at):
        even, odd = smooth[at]
        inner, inner_s = couple(even, odd, column_weight)
        outer, outer_s = couple(even, tuple(back(x) for x in odd), between)
        outer_next, outer_next_s = ahead(outer), ahead(outer_s)
        sides = ((outer, inner, outer_s + inner_s), (inner, outer_next, -inner_s - outer_next_s))
        first = []
        for j in range(2):
            up, up_s = upper[at][j]
            down, down_s = upper[at + 1][j]
            left, right, side_s = sides[j]
            scale = rcp(up + down + left + right + unwrap_damping)
            source = (up_s - down_s + side_s) * scale
            for k, value in enumerate((up, down, left, right)):
                coefs[at, 5 * j + k] = value * scale
            coefs[at, 5 * j + 4] = source
            first.append(source)
        return first

    def sweep(at, values):
        above, below = values[at - 1], values[at + 1]
        even, odd = values[at]
        beside = ((back(odd), odd), (even, ahead(even)))
        result = []
        for j in range(2):
            total = coefs[at, 5 * j + 4] + coefs[at, 5 * j] * above[j]
            total = total + coefs[at, 5 * j + 1] * below[j]
            total = total + coefs[at, 5 * j + 2] * beside[j][0]
            total = total + coefs[at, 5 * j + 3] * beside[j][1]
            result.append(total)
        return result

    window = [line(0), line(1)]
    for at in range(1, lines - 1):
        window.append(line(at + 1))
        smooth[at] = smooth_line(at, window)
        window.pop(0)
        if at >= 2:
            upper[at] = [couple(smooth[at][j], smooth[at - 1][j], None) for j in range(2)]
        if at >= 3:
            levels[1][at - 1] = stencil(at - 1)
        for level in range(2, SWEEPS + 1):
            row = at - level
            if 1 + level <= row <= lines - 2 - level:
                levels[level][row] = sweep(row, levels[level - 1])
                if level == SWEEPS:
                    for j in range(2):
                        phases[row - RIM, here, j * half : (j + 1) * half] = levels[level][row][j]


def solve_kernel(
    tiles, images, offsets, weight_hbm, out_hbm, formed, coefs, phases, weights, result, load_sem, save_sem
):
    lines, dates, double = images.shape
    columns = double // 2
    half = columns // 2
    per_date = offsets.shape[1]
    pairs = dates * per_date
    rows = phases.shape[0]
    loads = [
        pltpu.make_async_copy(weight_hbm.at[:, r], weights.at[r], load_sem.at[r])
        for r in range(rows)
    ]
    for load in loads:
        load.start()
    tile = lax.axis_index("tile")
    date = lax.axis_index("date")
    top = jnp.where(jnp.logical_and(tile == 0, date == 0), 0.0, 1.0)
    bottom = jnp.where(jnp.logical_and(tile == tiles - 1, date == 1), 0.0, 1.0)

    first = iota((pairs, 1), 0) // per_date
    first_pick = one_hot(iota((pairs, dates), 1) == first)
    of_date = mm(first_pick, offsets[...].astype(F32).astype(BF16))
    own = iota((pairs, per_date), 1) == iota((pairs, per_date), 0) % per_date
    offset = jnp.sum(jnp.where(own, of_date, 0.0), axis=1, keepdims=True)
    second = first + offset.astype(jnp.int32)
    second_pick = one_hot(iota((pairs, dates), 1) == second)
    valid = jnp.where(second < dates, 1.0 / 255.0, 0.0)

    def form(at, carry):
        image = images[at]
        a = mm(first_pick, image)
        b = mm(second_pick, image)
        a_re, a_im = a[:, :columns], a[:, columns:]
        b_re, b_im = b[:, :columns], b[:, columns:]
        formed[at, :, :columns] = a_re * b_re + a_im * b_im
        formed[at, :, columns:] = a_im * b_re - a_re * b_im
        return carry

    lax.fori_loop(0, lines, form, 0)

    block_pairs = 8

    def unwrap(block, carry):
        unwrap_block(block, block_pairs, formed, coefs, phases, top, bottom, half)
        return carry

    lax.fori_loop(0, pairs // block_pairs, unwrap, 0)

    for load in loads:
        load.wait()

    unknown = iota((pairs, dates), 1)
    covers = (unknown >= first) & (unknown < second) & (unknown < dates - 1)
    design = one_hot(covers)
    unknown_t = iota((dates, pairs), 0)
    first_t = iota((dates, pairs), 1) // per_date
    eye = iota((pairs, pairs), 0) == iota((pairs, pairs), 1)
    second_t = jnp.sum(jnp.where(eye, second.astype(F32), 0.0), axis=0, keepdims=True)
    covers_t = (unknown_t >= first_t) & (unknown_t < second_t.astype(jnp.int32))
    design_t = one_hot(covers_t & (unknown_t < dates - 1))
    design2 = jnp.concatenate([design, design], axis=1)
    design2_t = jnp.concatenate([design_t, design_t], axis=1)
    order = evens_first(columns)
    restore = one_hot(
        iota((columns, columns), 0)
        == (iota((columns, columns), 1) // 2 + (iota((columns, columns), 1) % 2) * half)
    )

    def forward(v):
        return mm(design2, jnp.concatenate(split(v), axis=0))

    def backward(x):
        return mm(design2_t, jnp.concatenate(split(x), axis=0))

    group = 4

    def invert(at, carry):
        lanes = range(group)
        index = [at * group + g for g in lanes]
        y = [phases[i] for i in index]
        base = [mm(weights[i].astype(F32).astype(BF16), order) * valid for i in index]
        v = [None] * group
        for pass_index in range(PASSES):
            left = [y[g] - forward(v[g]) if pass_index else y[g] for g in lanes]
            w = [
                base[g] * rcp(1.0 + left[g] * left[g] * (1.0 / residual_scale**2))
                for g in lanes
            ]
            scale = [
                (1.0 / SPAN) * rcp(backward(w[g]) + solve_damping) for g in lanes
            ]
            for step_index in range(STEPS):
                if step_index:
                    left = [y[g] - forward(v[g]) for g in lanes]
                gradient = [backward(w[g] * left[g]) for g in lanes]
                for g in lanes:
                    if v[g] is None:
                        v[g] = gradient[g] * scale[g]
                    else:
                        v[g] = v[g] + (gradient[g] - solve_damping * v[g]) * scale[g]
        for g in lanes:
            high, rest = split(v[g])
            middle, low = split(v[g] - high.astype(F32))
            full = mm(high, restore) + (mm(middle, restore) + mm(low, restore))
            result[index[g]] = full[: dates - 1]
        return carry

    lax.fori_loop(0, rows // group, invert, 0)
    saves = [
        pltpu.make_async_copy(result.at[r], out_hbm.at[:, r], save_sem.at[r])
        for r in range(rows)
    ]
    for save in saves:
        save.start()
    for save in saves:
        save.wait()


def solve(images, pair_offset, pair_weight, tiles):
    lines, dates, double = images.shape
    columns = double // 2
    pairs, rows = pair_weight.shape[:2]
    whole = pl.BlockSpec(memory_space=pltpu.VMEM)
    return pl.pallas_call(
        functools.partial(solve_kernel, tiles),
        out_shape=jax.ShapeDtypeStruct((dates - 1, rows, columns), F32),
        in_specs=[whole, whole, pl.BlockSpec(memory_space=pl.ANY)],
        out_specs=pl.BlockSpec(memory_space=pl.ANY),
        scratch_shapes=[
            pltpu.VMEM((lines, pairs, double), F32),
            pltpu.VMEM((lines, 10, 8, columns // 2), F32),
            pltpu.VMEM((rows, pairs, columns), F32),
            pltpu.VMEM((rows, pairs, columns), jnp.int32),
            pltpu.VMEM((rows, dates - 1, columns), F32),
            pltpu.SemaphoreType.DMA((rows,)),
            pltpu.SemaphoreType.DMA((rows,)),
        ],
        compiler_params=pltpu.CompilerParams(vmem_limit_bytes=40 << 20),
    )(images, pair_offset, pair_weight)


def local(slc_real, slc_imag, pair_offset, pair_weight, tiles):
    images = exchange(slc_real, slc_imag, tiles)
    return solve(images, pair_offset, pair_weight, tiles)


def solution(mesh):
    placed = (
        P("date", ("scene", "tile"), None),
        P("date", ("scene", "tile"), None),
        P(),
        P(None, ("scene", "tile", "date"), None),
    )
    return jax.shard_map(
        functools.partial(local, tiles=mesh.shape["tile"]),
        mesh=mesh,
        in_specs=placed,
        out_specs=P(None, ("scene", "tile", "date"), None),
        check_vma=False,
    )
```

time: 172 us -> 56.4 us (0.33)
  the two profiles are of different devices: /device:TPU:13 before, /device:TPU:19 now
where the time goes in v1:
time: 56.4 us; the launch traced here: 56.2 us
  Pallas kernels  51.9 us (92%)
  local copies, waits for them, and re-layouts  4.25 us (8%)
    pallas_call x1, Pallas kernels, solve(): pl.pallas_call(functools.partial(solve_kernel, tiles), out_shape=jax.Shap...  41.6 us
    pallas_call x1, Pallas kernels, exchange(): pl.pallas_call(functools.partial(exchange_kernel, tiles), out_shape=jax.S...  10.3 us
    unnamed x7, local copies, waits for them, and re-layouts  4.25 us

profile of v1, /device:TPU:19, one launch (start us, length us, event | category | flops | bytes accessed | tf_op | source)
XLA Modules:
  0.0 56.2 jit_solution(7065448398304255494)
XLA Ops:
  0.0 0.8 %copy.5.offsets = s32[32,4]{1,0:T(8,128)S(1)} copy(s32[32,4]{0,1:T(4,128)} %param.6) | data formatting | bytes 1024 | tf_op args[2]
  0.8 0.0 copy-start.1
  0.8 0.9 %copy-done.1 = bf16[16,32,256]{2,1,0:T(8,128)(2,1)S(1)} copy-done((bf16[16,32,256]{2,1,0:T(8,128)(2,1)S(1)}, bf16[16,32,256]{2,1,0:T(8,128)(2,1)}, u32[]{:S(2)}) %copy-start.1) | copy-done | bytes 262168
  1.7 0.0 copy-start.2
  1.7 0.9 %copy-done.2 = bf16[16,32,256]{2,1,0:T(8,128)(2,1)S(1)} copy-done((bf16[16,32,256]{2,1,0:T(8,128)(2,1)S(1)}, bf16[16,32,256]{2,1,0:T(8,128)(2,1)}, u32[]{:S(2)}) %copy-start.2) | copy-done | bytes 262168
  2.7 10.3 %shard_map.46.images = bf16[34,32,512]{2,1,0:T(8,128)(2,1)S(1)} custom-call(bf16[16,32,256]{2,1,0:T(8,128)(2,1)S(1)} %copy-done.1, bf16[16,32,256]{2,1,0:T(8,128)(2,1)S(1)} %copy-done.2), custom_call_target="tpu_custom_call" | custom-call | tf_op jit(solution)/shard_map/pallas_call | solution.py:176
  13.0 0.0 copy-start
  13.0 1.6 %copy-done = s32[128,16,256]{2,1,0:T(8,128)S(1)} copy-done((s32[128,16,256]{2,1,0:T(8,128)S(1)}, s32[128,16,256]{2,1,0:T(8,128)}, u32[]{:S(2)}) %copy-start) | copy-done | bytes 2097176
  14.5 41.6 %shard_map.47 = f32[31,16,256]{2,1,0:T(8,128)} custom-call(bf16[34,32,512]{2,1,0:T(8,128)(2,1)S(1)} %shard_map.46.images, s32[32,4]{1,0:T(8,128)S(1)} %copy.5.offsets, s32[128,16,256]{2,1,0:T(8,128)S(1)} %copy-done), custom_call_target="tpu_custom_call" | custom-call | tf_op jit(solution)/shard_map/pallas_call | solution.py:411
Async XLA Ops:
  0.8 0.9 %copy-start.1 = (bf16[16,32,256]{2,1,0:T(8,128)(2,1)S(1)}, bf16[16,32,256]{2,1,0:T(8,128)(2,1)}, u32[]{:S(2)}) copy-start(bf16[16,32,256]{2,1,0:T(8,128)(2,1)} %re_ref.1) | copy-start | bytes 786436
  1.7 0.9 %copy-start.2 = (bf16[16,32,256]{2,1,0:T(8,128)(2,1)S(1)}, bf16[16,32,256]{2,1,0:T(8,128)(2,1)}, u32[]{:S(2)}) copy-start(bf16[16,32,256]{2,1,0:T(8,128)(2,1)} %im_ref.1) | copy-start | bytes 786436
  13.0 1.6 %copy-start = (s32[128,16,256]{2,1,0:T(8,128)S(1)}, s32[128,16,256]{2,1,0:T(8,128)}, u32[]{:S(2)}) copy-start(s32[128,16,256]{2,1,0:T(8,128)} %weight_hbm.1) | copy-start | bytes 6291460

commit v2 on v1

--- a/solution.py
+++ b/solution.py
@@ -36,8 +36,7 @@
 
 
 def rcp(x):
-    r = pl.reciprocal(x, approx=True)
-    return r * (2.0 - x * r)
+    return pl.reciprocal(x, approx=True)
 
 
 def split(x):
@@ -52,8 +51,16 @@
     return one_hot(iota((columns, columns), 0) == old)
 
 
-def exchange_kernel(tiles, re_ref, im_ref, out_ref, send_ref, send_sem, recv_sem):
-    dates, tile_rows, columns = re_ref.shape
+def exchange_kernel(
+    tiles, re_hbm, im_hbm, out_ref, parts_ref, send_ref, zeros, load_sem, send_sem, recv_sem
+):
+    dates, tile_rows, columns = re_hbm.shape
+    loads = [
+        pltpu.make_async_copy(hbm, parts_ref.at[part], load_sem.at[part])
+        for part, hbm in enumerate((re_hbm, im_hbm))
+    ]
+    for load in loads:
+        load.start()
     shard = tile_rows // 2
     scene = lax.axis_index("scene")
     tile = lax.axis_index("tile")
@@ -82,21 +89,26 @@
 
     order = evens_first(columns)
     count = dates * tile_rows
-    new = iota((count, 1), 0)
-    old = (new % dates) * tile_rows + new // dates
-    rows_first = one_hot(iota((count, count), 1) == old)
-    for part, ref in enumerate((re_ref, im_ref)):
-        flat = ref[...].reshape(count, columns)
-        moved = mm(rows_first, mm(flat, order).astype(BF16)).astype(BF16)
-        send_ref[:, :, part * columns : (part + 1) * columns] = moved.reshape(
-            tile_rows, dates, columns
-        )
+
+    def arrange(start, size):
+        new = iota((size * dates, 1), 0) + start * dates
+        old = (new % dates) * tile_rows + new // dates
+        pick = one_hot(iota((size * dates, count), 1) == old)
+        for part in range(2):
+            moved = mm(pick, parts_ref[part].reshape(count, columns)).astype(BF16)
+            send_ref[start : start + size, :, part * columns : (part + 1) * columns] = (
+                mm(moved, order).astype(BF16).reshape(size, dates, columns)
+            )
+
+    for load in loads:
+        load.wait()
+    arrange(0, RIM)
+    arrange(tile_rows - RIM, RIM)
 
     pl.semaphore_wait(barrier, 1 + has_up.astype(jnp.int32) + has_down.astype(jnp.int32))
 
     span = shard + RIM
     mine = pl.ds(pl.multiple_of(date * dates, dates), dates)
-    theirs = pl.ds(pl.multiple_of(other * dates, dates), dates)
 
     def copy(source, target, to_tile, to_date, send_at, recv_at):
         return pltpu.make_async_remote_copy(
@@ -129,12 +141,15 @@
     def _():
         down_copy.start()
 
+    arrange(RIM, tile_rows - 2 * RIM)
     across.start()
 
-    out_ref[pl.ds((1 - date) * RIM, span), mine] = send_ref[
-        pl.ds(date * (tile_rows - span), span)
-    ]
-    beyond = date * span
+    keep = pltpu.make_async_copy(
+        send_ref.at[pl.ds(date * (tile_rows - span), span)],
+        out_ref.at[pl.ds((1 - date) * RIM, span), mine],
+        load_sem.at[0],
+    )
+    keep.start()
     missing = jnp.logical_or(
         jnp.logical_and(date == 0, tile == 0),
         jnp.logical_and(date == 1, tile == tiles - 1),
@@ -142,8 +157,14 @@
 
     @pl.when(missing)
     def _():
-        out_ref[pl.ds(beyond, RIM)] = jnp.zeros((RIM, 2 * dates, 2 * columns), BF16)
-
+        zeros[...] = jnp.zeros(zeros.shape, BF16)
+        clear = pltpu.make_async_copy(
+            zeros, out_ref.at[pl.ds(date * span, RIM)], load_sem.at[1]
+        )
+        clear.start()
+        clear.wait()
+
+    keep.wait()
     across.wait_send()
 
     @pl.when(has_up)
@@ -172,19 +193,21 @@
 def exchange(slc_real, slc_imag, tiles):
     dates, tile_rows, columns = slc_real.shape
     shape = (tile_rows // 2 + 2 * RIM, 2 * dates, 2 * columns)
-    whole = pl.BlockSpec(memory_space=pltpu.VMEM)
     return pl.pallas_call(
         functools.partial(exchange_kernel, tiles),
         out_shape=jax.ShapeDtypeStruct(shape, BF16),
-        in_specs=[whole, whole],
-        out_specs=whole,
+        in_specs=[pl.BlockSpec(memory_space=pl.ANY)] * 2,
+        out_specs=pl.BlockSpec(memory_space=pl.ANY),
         scratch_shapes=[
+            pltpu.VMEM((2, dates, tile_rows, columns), BF16),
             pltpu.VMEM((tile_rows, dates, 2 * columns), BF16),
+            pltpu.VMEM((RIM, 2 * dates, 2 * columns), BF16),
+            pltpu.SemaphoreType.DMA((2,)),
             pltpu.SemaphoreType.DMA((3,)),
             pltpu.SemaphoreType.DMA((3,)),
         ],
         compiler_params=pltpu.CompilerParams(
-            collective_id=0, has_side_effects=True, vmem_limit_bytes=24 << 20
+            collective_id=0, has_side_effects=True, vmem_limit_bytes=(64 << 20) - 1280 * 1024
         ),
     )(slc_real, slc_imag)
 
@@ -259,40 +282,54 @@
         beside = ((back(odd), odd), (even, ahead(even)))
         result = []
         for j in range(2):
-            total = coefs[at, 5 * j + 4] + coefs[at, 5 * j] * above[j]
-            total = total + coefs[at, 5 * j + 1] * below[j]
-            total = total + coefs[at, 5 * j + 2] * beside[j][0]
-            total = total + coefs[at, 5 * j + 3] * beside[j][1]
+            vertical = coefs[at, 5 * j] * above[j] + coefs[at, 5 * j + 1] * below[j]
+            sides = coefs[at, 5 * j + 2] * beside[j][0] + coefs[at, 5 * j + 3] * beside[j][1]
+            total = (coefs[at, 5 * j + 4] + vertical) + sides
             result.append(total)
         return result
 
     window = [line(0), line(1)]
-    for at in range(1, lines - 1):
-        window.append(line(at + 1))
-        smooth[at] = smooth_line(at, window)
-        window.pop(0)
-        if at >= 2:
-            upper[at] = [couple(smooth[at][j], smooth[at - 1][j], None) for j in range(2)]
-        if at >= 3:
-            levels[1][at - 1] = stencil(at - 1)
-        for level in range(2, SWEEPS + 1):
-            row = at - level
+    for step in range(1, lines + SWEEPS):
+        for level in range(SWEEPS, 1, -1):
+            row = step - 1 - 2 * level
             if 1 + level <= row <= lines - 2 - level:
-                levels[level][row] = sweep(row, levels[level - 1])
+                values = sweep(row, levels[level - 1])
+                levels[level][row] = values
                 if level == SWEEPS:
                     for j in range(2):
-                        phases[row - RIM, here, j * half : (j + 1) * half] = levels[level][row][j]
+                        phases[row - RIM, here, j * half : (j + 1) * half] = values[j]
+        if 2 <= step - 3 <= lines - 3:
+            levels[1][step - 3] = stencil(step - 3)
+        if 2 <= step - 1 <= lines - 2:
+            upper[step - 1] = [
+                couple(smooth[step - 1][j], smooth[step - 2][j], None) for j in range(2)
+            ]
+        if step <= lines - 2:
+            window.append(line(step + 1))
+            smooth[step] = smooth_line(step, window)
+            window.pop(0)
 
 
 def solve_kernel(
-    tiles, images, offsets, weight_hbm, out_hbm, formed, coefs, phases, weights, result, load_sem, save_sem
+    tiles, images_hbm, offsets, weight_hbm, out_hbm, images, formed, coefs, phases, weights, result, line_sem, load_sem, save_sem
 ):
-    lines, dates, double = images.shape
+    lines, dates, double = images_hbm.shape
     columns = double // 2
     half = columns // 2
-    per_date = offsets.shape[1]
+    per_date = offsets.shape[0]
     pairs = dates * per_date
     rows = phases.shape[0]
+    chunk = 4
+    fetches = [
+        pltpu.make_async_copy(
+            images_hbm.at[pl.ds(at, min(chunk, lines - at))],
+            images.at[pl.ds(at, min(chunk, lines - at))],
+            line_sem.at[at // chunk],
+        )
+        for at in range(0, lines, chunk)
+    ]
+    for fetch in fetches:
+        fetch.start()
     loads = [
         pltpu.make_async_copy(weight_hbm.at[:, r], weights.at[r], load_sem.at[r])
         for r in range(rows)
@@ -306,14 +343,19 @@
 
     first = iota((pairs, 1), 0) // per_date
     first_pick = one_hot(iota((pairs, dates), 1) == first)
-    of_date = mm(first_pick, offsets[...].astype(F32).astype(BF16))
+    of_date = lax.dot_general(
+        first_pick,
+        offsets[...].astype(F32).astype(BF16),
+        (((1,), (1,)), ((), ())),
+        preferred_element_type=F32,
+    )
     own = iota((pairs, per_date), 1) == iota((pairs, per_date), 0) % per_date
     offset = jnp.sum(jnp.where(own, of_date, 0.0), axis=1, keepdims=True)
     second = first + offset.astype(jnp.int32)
     second_pick = one_hot(iota((pairs, dates), 1) == second)
     valid = jnp.where(second < dates, 1.0 / 255.0, 0.0)
 
-    def form(at, carry):
+    def form(at):
         image = images[at]
         a = mm(first_pick, image)
         b = mm(second_pick, image)
@@ -321,9 +363,11 @@
         b_re, b_im = b[:, :columns], b[:, columns:]
         formed[at, :, :columns] = a_re * b_re + a_im * b_im
         formed[at, :, columns:] = a_im * b_re - a_re * b_im
-        return carry
-
-    lax.fori_loop(0, lines, form, 0)
+
+    for at in range(lines):
+        if at % chunk == 0:
+            fetches[at // chunk].wait()
+        form(at)
 
     block_pairs = 8
 
@@ -359,7 +403,7 @@
     def backward(x):
         return mm(design2_t, jnp.concatenate(split(x), axis=0))
 
-    group = 4
+    group = 8 if rows % 8 == 0 else 1
 
     def invert(at, carry):
         lanes = range(group)
@@ -411,24 +455,26 @@
     return pl.pallas_call(
         functools.partial(solve_kernel, tiles),
         out_shape=jax.ShapeDtypeStruct((dates - 1, rows, columns), F32),
-        in_specs=[whole, whole, pl.BlockSpec(memory_space=pl.ANY)],
+        in_specs=[pl.BlockSpec(memory_space=pl.ANY), whole, pl.BlockSpec(memory_space=pl.ANY)],
         out_specs=pl.BlockSpec(memory_space=pl.ANY),
         scratch_shapes=[
+            pltpu.VMEM(images.shape, BF16),
             pltpu.VMEM((lines, pairs, double), F32),
             pltpu.VMEM((lines, 10, 8, columns // 2), F32),
             pltpu.VMEM((rows, pairs, columns), F32),
             pltpu.VMEM((rows, pairs, columns), jnp.int32),
             pltpu.VMEM((rows, dates - 1, columns), F32),
+            pltpu.SemaphoreType.DMA((lines,)),
             pltpu.SemaphoreType.DMA((rows,)),
             pltpu.SemaphoreType.DMA((rows,)),
         ],
-        compiler_params=pltpu.CompilerParams(vmem_limit_bytes=40 << 20),
+        compiler_params=pltpu.CompilerParams(vmem_limit_bytes=(64 << 20) - 1280 * 1024),
     )(images, pair_offset, pair_weight)
 
 
 def local(slc_real, slc_imag, pair_offset, pair_weight, tiles):
     images = exchange(slc_real, slc_imag, tiles)
-    return solve(images, pair_offset, pair_weight, tiles)
+    return solve(images, pair_offset.T, pair_weight, tiles)
 
 
 def solution(mesh):

time: 56.4 us -> 45.5 us (0.81)
  Pallas kernels: 51.9 us -> 45.4 us
  local copies, waits for them, and re-layouts: 4.25 us -> 0 us
    pallas_call x1, Pallas kernels: 41.6 us -> 34.8 us  [solve(): pl.pallas_call(functools.partial(solve_kernel, tiles), out_shape=jax.Shap...]
    unnamed x7 -> x0, local copies, waits for them, and re-layouts: 4.25 us -> none
where the time goes in v2:
time: 45.5 us; the launch traced here: 45.4 us
  Pallas kernels  45.4 us (100%)
    pallas_call x1, Pallas kernels, solve(): pl.pallas_call(functools.partial(solve_kernel, tiles), out_shape=jax.Shap...  34.8 us
    pallas_call x1, Pallas kernels, exchange(): pl.pallas_call(functools.partial(exchange_kernel, tiles), out_shape=jax.S...  10.6 us

profile of v2, /device:TPU:19, one launch (start us, length us, event | category | flops | bytes accessed | tf_op | source)
XLA Modules:
  0.0 45.4 jit_solution(16327133234442534311)
XLA Ops:
  0.0 10.6 %shard_map.46.images_hbm = bf16[34,32,512]{2,1,0:T(8,128)(2,1)} custom-call(bf16[16,32,256]{2,1,0:T(8,128)(2,1)} %re_hbm.1, bf16[16,32,256]{2,1,0:T(8,128)(2,1)} %im_hbm.1), custom_call_target="tpu_custom_call" | custom-call | tf_op jit(solution)/shard_map/pallas_call | solution.py:196
  10.6 34.8 %shard_map.47 = f32[31,16,256]{2,1,0:T(8,128)} custom-call(bf16[34,32,512]{2,1,0:T(8,128)(2,1)} %shard_map.46.images_hbm, s32[4,32]{1,0:T(4,128)} %bitcast.1, s32[128,16,256]{2,1,0:T(8,128)} %weight_hbm.1), custom_call_target="tpu_custom_call" | custom-call | tf_op jit(solution)/shard_map/pallas_call | solution.py:455

commit v3 on v2

--- a/solution.py
+++ b/solution.py
@@ -212,7 +212,7 @@
     )(slc_real, slc_imag)
 
 
-def unwrap_block(block, pairs, formed, coefs, phases, top, bottom, half):
+def stencil_block(block, pairs, formed, coefs, top, bottom, half):
     lines = formed.shape[0]
     here = pl.ds(pl.multiple_of(block * pairs, pairs), pairs)
     lane = iota((pairs, half), 1)
@@ -227,7 +227,6 @@
 
     smooth = {}
     upper = {}
-    levels = [dict() for _ in range(SWEEPS + 1)]
 
     def smooth_line(at, rows):
         result = []
@@ -263,18 +262,34 @@
         outer, outer_s = couple(even, tuple(back(x) for x in odd), between)
         outer_next, outer_next_s = ahead(outer), ahead(outer_s)
         sides = ((outer, inner, outer_s + inner_s), (inner, outer_next, -inner_s - outer_next_s))
-        first = []
         for j in range(2):
             up, up_s = upper[at][j]
             down, down_s = upper[at + 1][j]
             left, right, side_s = sides[j]
             scale = rcp(up + down + left + right + unwrap_damping)
-            source = (up_s - down_s + side_s) * scale
-            for k, value in enumerate((up, down, left, right)):
-                coefs[at, 5 * j + k] = value * scale
-            coefs[at, 5 * j + 4] = source
-            first.append(source)
-        return first
+            source = up_s - down_s + side_s
+            for k, value in enumerate((up, down, left, right, source)):
+                coefs[at, 5 * j + k, here] = value * scale
+
+    window = [line(0), line(1)]
+    for step in range(1, lines + 1):
+        if 2 <= step - 3 <= lines - 3:
+            stencil(step - 3)
+        if 2 <= step - 1 <= lines - 2:
+            upper[step - 1] = [
+                couple(smooth[step - 1][j], smooth[step - 2][j], None) for j in range(2)
+            ]
+        if step <= lines - 2:
+            window.append(line(step + 1))
+            smooth[step] = smooth_line(step, window)
+            window.pop(0)
+
+
+def sweep_block(block, pairs, lines, coefs, phases, half):
+    here = pl.ds(pl.multiple_of(block * pairs, pairs), pairs)
+    back = lambda x: pltpu.roll(x, 1, 1)
+    ahead = lambda x: pltpu.roll(x, half - 1, 1)
+    levels = [dict() for _ in range(SWEEPS + 1)]
 
     def sweep(at, values):
         above, below = values[at - 1], values[at + 1]
@@ -282,14 +297,13 @@
         beside = ((back(odd), odd), (even, ahead(even)))
         result = []
         for j in range(2):
-            vertical = coefs[at, 5 * j] * above[j] + coefs[at, 5 * j + 1] * below[j]
-            sides = coefs[at, 5 * j + 2] * beside[j][0] + coefs[at, 5 * j + 3] * beside[j][1]
-            total = (coefs[at, 5 * j + 4] + vertical) + sides
+            vertical = coefs[at, 5 * j, here] * above[j] + coefs[at, 5 * j + 1, here] * below[j]
+            sides = coefs[at, 5 * j + 2, here] * beside[j][0] + coefs[at, 5 * j + 3, here] * beside[j][1]
+            total = (coefs[at, 5 * j + 4, here] + vertical) + sides
             result.append(total)
         return result
 
-    window = [line(0), line(1)]
-    for step in range(1, lines + SWEEPS):
+    for step in range(5, lines + SWEEPS):
         for level in range(SWEEPS, 1, -1):
             row = step - 1 - 2 * level
             if 1 + level <= row <= lines - 2 - level:
@@ -299,15 +313,7 @@
                     for j in range(2):
                         phases[row - RIM, here, j * half : (j + 1) * half] = values[j]
         if 2 <= step - 3 <= lines - 3:
-            levels[1][step - 3] = stencil(step - 3)
-        if 2 <= step - 1 <= lines - 2:
-            upper[step - 1] = [
-                couple(smooth[step - 1][j], smooth[step - 2][j], None) for j in range(2)
-            ]
-        if step <= lines - 2:
-            window.append(line(step + 1))
-            smooth[step] = smooth_line(step, window)
-            window.pop(0)
+            levels[1][step - 3] = [coefs[step - 3, 5 * j + 4, here] for j in range(2)]
 
 
 def solve_kernel(
@@ -371,10 +377,15 @@
 
     block_pairs = 8
 
+    def build(block, carry):
+        stencil_block(block, block_pairs, formed, coefs, top, bottom, half)
+        return carry
+
     def unwrap(block, carry):
-        unwrap_block(block, block_pairs, formed, coefs, phases, top, bottom, half)
+        sweep_block(block, block_pairs, lines, coefs, phases, half)
         return carry
 
+    lax.fori_loop(0, pairs // block_pairs, build, 0)
     lax.fori_loop(0, pairs // block_pairs, unwrap, 0)
 
     for load in loads:
@@ -434,17 +445,15 @@
             middle, low = split(v[g] - high.astype(F32))
             full = mm(high, restore) + (mm(middle, restore) + mm(low, restore))
             result[index[g]] = full[: dates - 1]
+            save(index[g]).start()
         return carry
 
+    def save(r):
+        return pltpu.make_async_copy(result.at[r], out_hbm.at[:, r], save_sem.at[r])
+
     lax.fori_loop(0, rows // group, invert, 0)
-    saves = [
-        pltpu.make_async_copy(result.at[r], out_hbm.at[:, r], save_sem.at[r])
-        for r in range(rows)
-    ]
-    for save in saves:
-        save.start()
-    for save in saves:
-        save.wait()
+    for r in range(rows):
+        save(r).wait()
 
 
 def solve(images, pair_offset, pair_weight, tiles):
@@ -460,7 +469,7 @@
         scratch_shapes=[
             pltpu.VMEM(images.shape, BF16),
             pltpu.VMEM((lines, pairs, double), F32),
-            pltpu.VMEM((lines, 10, 8, columns // 2), F32),
+            pltpu.VMEM((lines, 10, pairs, columns // 2), F32),
             pltpu.VMEM((rows, pairs, columns), F32),
             pltpu.VMEM((rows, pairs, columns), jnp.int32),
             pltpu.VMEM((rows, dates - 1, columns), F32),

time: 45.5 us -> 53.6 us (1.18)
  Pallas kernels: 45.4 us -> 53.5 us
    pallas_call x1, Pallas kernels: 34.8 us -> 42.9 us  [solve(): pl.pallas_call(functools.partial(solve_kernel, tiles), out_shape=jax.Shap...]
where the time goes in v3:
time: 53.6 us; the launch traced here: 53.5 us
  Pallas kernels  53.5 us (100%)
    pallas_call x1, Pallas kernels, solve(): pl.pallas_call(functools.partial(solve_kernel, tiles), out_shape=jax.Shap...  42.9 us
    pallas_call x1, Pallas kernels, exchange(): pl.pallas_call(functools.partial(exchange_kernel, tiles), out_shape=jax.S...  10.6 us

profile of v3, /device:TPU:19, one launch (start us, length us, event | category | flops | bytes accessed | tf_op | source)
XLA Modules:
  0.0 53.5 jit_solution(514643231547327183)
XLA Ops:
  0.0 10.6 %shard_map.46.images_hbm = bf16[34,32,512]{2,1,0:T(8,128)(2,1)} custom-call(bf16[16,32,256]{2,1,0:T(8,128)(2,1)} %re_hbm.1, bf16[16,32,256]{2,1,0:T(8,128)(2,1)} %im_hbm.1), custom_call_target="tpu_custom_call" | custom-call | tf_op jit(solution)/shard_map/pallas_call | solution.py:196
  10.6 42.9 %shard_map.47 = f32[31,16,256]{2,1,0:T(8,128)} custom-call(bf16[34,32,512]{2,1,0:T(8,128)(2,1)} %shard_map.46.images_hbm, s32[4,32]{1,0:T(4,128)} %bitcast.1, s32[128,16,256]{2,1,0:T(8,128)} %weight_hbm.1), custom_call_target="tpu_custom_call" | custom-call | tf_op jit(solution)/shard_map/pallas_call | solution.py:464

commit v4 on v2

--- a/solution.py
+++ b/solution.py
@@ -227,6 +227,7 @@
 
     smooth = {}
     upper = {}
+    roots = {}
     levels = [dict() for _ in range(SWEEPS + 1)]
 
     def smooth_line(at, rows):
@@ -263,29 +264,33 @@
         outer, outer_s = couple(even, tuple(back(x) for x in odd), between)
         outer_next, outer_next_s = ahead(outer), ahead(outer_s)
         sides = ((outer, inner, outer_s + inner_s), (inner, outer_next, -inner_s - outer_next_s))
-        first = []
+        root = []
+        source = []
         for j in range(2):
             up, up_s = upper[at][j]
             down, down_s = upper[at + 1][j]
             left, right, side_s = sides[j]
-            scale = rcp(up + down + left + right + unwrap_damping)
-            source = (up_s - down_s + side_s) * scale
-            for k, value in enumerate((up, down, left, right)):
-                coefs[at, 5 * j + k] = value * scale
-            coefs[at, 5 * j + 4] = source
-            first.append(source)
-        return first
+            root.append(lax.rsqrt(up + down + left + right + unwrap_damping))
+            source.append((up_s - down_s + side_s) * root[j])
+            if at - 1 in roots:
+                coefs[at, j] = up * (root[j] * roots[at - 1][j])
+            coefs[at, 4 + j] = source[j]
+            if RIM <= at < lines - RIM:
+                coefs[at, 6 + j] = root[j]
+        coefs[at, 2] = inner * (root[0] * root[1])
+        coefs[at, 3] = outer * (root[0] * back(root[1]))
+        roots[at] = root
+        return source
 
     def sweep(at, values):
         above, below = values[at - 1], values[at + 1]
         even, odd = values[at]
-        beside = ((back(odd), odd), (even, ahead(even)))
+        inner, outer = coefs[at, 2], coefs[at, 3]
+        beside = (inner * odd + outer * back(odd), inner * even + ahead(outer * even))
         result = []
         for j in range(2):
-            vertical = coefs[at, 5 * j] * above[j] + coefs[at, 5 * j + 1] * below[j]
-            sides = coefs[at, 5 * j + 2] * beside[j][0] + coefs[at, 5 * j + 3] * beside[j][1]
-            total = (coefs[at, 5 * j + 4] + vertical) + sides
-            result.append(total)
+            vertical = coefs[at, j] * above[j] + coefs[at + 1, j] * below[j]
+            result.append((coefs[at, 4 + j] + vertical) + beside[j])
         return result
 
     window = [line(0), line(1)]
@@ -297,7 +302,9 @@
                 levels[level][row] = values
                 if level == SWEEPS:
                     for j in range(2):
-                        phases[row - RIM, here, j * half : (j + 1) * half] = values[j]
+                        phases[row - RIM, here, j * half : (j + 1) * half] = (
+                            values[j] * coefs[row, 6 + j]
+                        )
         if 2 <= step - 3 <= lines - 3:
             levels[1][step - 3] = stencil(step - 3)
         if 2 <= step - 1 <= lines - 2:
@@ -434,17 +441,15 @@
             middle, low = split(v[g] - high.astype(F32))
             full = mm(high, restore) + (mm(middle, restore) + mm(low, restore))
             result[index[g]] = full[: dates - 1]
+            save(index[g]).start()
         return carry
 
+    def save(r):
+        return pltpu.make_async_copy(result.at[r], out_hbm.at[:, r], save_sem.at[r])
+
     lax.fori_loop(0, rows // group, invert, 0)
-    saves = [
-        pltpu.make_async_copy(result.at[r], out_hbm.at[:, r], save_sem.at[r])
-        for r in range(rows)
-    ]
-    for save in saves:
-        save.start()
-    for save in saves:
-        save.wait()
+    for r in range(rows):
+        save(r).wait()
 
 
 def solve(images, pair_offset, pair_weight, tiles):
@@ -460,7 +465,7 @@
         scratch_shapes=[
             pltpu.VMEM(images.shape, BF16),
             pltpu.VMEM((lines, pairs, double), F32),
-            pltpu.VMEM((lines, 10, 8, columns // 2), F32),
+            pltpu.VMEM((lines, 8, 8, columns // 2), F32),
             pltpu.VMEM((rows, pairs, columns), F32),
             pltpu.VMEM((rows, pairs, columns), jnp.int32),
             pltpu.VMEM((rows, dates - 1, columns), F32),

time: 45.5 us -> 50 us (1.099)
  Pallas kernels: 45.4 us -> 49.8 us
    pallas_call x1, Pallas kernels: 34.8 us -> 39.3 us  [solve(): pl.pallas_call(functools.partial(solve_kernel, tiles), out_shape=jax.Shap...]
where the time goes in v4:
time: 50 us; the launch traced here: 49.8 us
  Pallas kernels  49.8 us (100%)
    pallas_call x1, Pallas kernels, solve(): pl.pallas_call(functools.partial(solve_kernel, tiles), out_shape=jax.Shap...  39.3 us
    pallas_call x1, Pallas kernels, exchange(): pl.pallas_call(functools.partial(exchange_kernel, tiles), out_shape=jax.S...  10.6 us

profile of v4, /device:TPU:19, one launch (start us, length us, event | category | flops | bytes accessed | tf_op | source)
XLA Modules:
  0.0 49.8 jit_solution(2066561965021691237)
XLA Ops:
  0.0 10.6 %shard_map.46.images_hbm = bf16[34,32,512]{2,1,0:T(8,128)(2,1)} custom-call(bf16[16,32,256]{2,1,0:T(8,128)(2,1)} %re_hbm.1, bf16[16,32,256]{2,1,0:T(8,128)(2,1)} %im_hbm.1), custom_call_target="tpu_custom_call" | custom-call | tf_op jit(solution)/shard_map/pallas_call | solution.py:196
  10.6 39.3 %shard_map.47 = f32[31,16,256]{2,1,0:T(8,128)} custom-call(bf16[34,32,512]{2,1,0:T(8,128)(2,1)} %shard_map.46.images_hbm, s32[4,32]{1,0:T(4,128)} %bitcast.1, s32[128,16,256]{2,1,0:T(8,128)} %weight_hbm.1), custom_call_target="tpu_custom_call" | custom-call | tf_op jit(solution)/shard_map/pallas_call | solution.py:460

commit v5 on v4

--- a/solution.py
+++ b/solution.py
@@ -326,7 +326,7 @@
     per_date = offsets.shape[0]
     pairs = dates * per_date
     rows = phases.shape[0]
-    chunk = 4
+    chunk = (lines + 1) // 2
     fetches = [
         pltpu.make_async_copy(
             images_hbm.at[pl.ds(at, min(chunk, lines - at))],
@@ -441,13 +441,14 @@
             middle, low = split(v[g] - high.astype(F32))
             full = mm(high, restore) + (mm(middle, restore) + mm(low, restore))
             result[index[g]] = full[: dates - 1]
-            save(index[g]).start()
         return carry
 
     def save(r):
         return pltpu.make_async_copy(result.at[r], out_hbm.at[:, r], save_sem.at[r])
 
     lax.fori_loop(0, rows // group, invert, 0)
+    for r in range(rows):
+        save(r).start()
     for r in range(rows):
         save(r).wait()
 

time: 50 us -> 49.3 us (0.986)
  Pallas kernels: 49.8 us -> 49.2 us
    pallas_call x1, Pallas kernels: 39.3 us -> 38.6 us  [solve(): pl.pallas_call(functools.partial(solve_kernel, tiles), out_shape=jax.Shap...]
where the time goes in v5:
time: 49.3 us; the launch traced here: 49.2 us
  Pallas kernels  49.2 us (100%)
    pallas_call x1, Pallas kernels, solve(): pl.pallas_call(functools.partial(solve_kernel, tiles), out_shape=jax.Shap...  38.6 us
    pallas_call x1, Pallas kernels, exchange(): pl.pallas_call(functools.partial(exchange_kernel, tiles), out_shape=jax.S...  10.6 us

profile of v5, /device:TPU:19, one launch (start us, length us, event | category | flops | bytes accessed | tf_op | source)
XLA Modules:
  0.0 49.2 jit_solution(12257861326943829514)
XLA Ops:
  0.0 10.6 %shard_map.46.images_hbm = bf16[34,32,512]{2,1,0:T(8,128)(2,1)} custom-call(bf16[16,32,256]{2,1,0:T(8,128)(2,1)} %re_hbm.1, bf16[16,32,256]{2,1,0:T(8,128)(2,1)} %im_hbm.1), custom_call_target="tpu_custom_call" | custom-call | tf_op jit(solution)/shard_map/pallas_call | solution.py:196
  10.6 38.6 %shard_map.47 = f32[31,16,256]{2,1,0:T(8,128)} custom-call(bf16[34,32,512]{2,1,0:T(8,128)(2,1)} %shard_map.46.images_hbm, s32[4,32]{1,0:T(4,128)} %bitcast.1, s32[128,16,256]{2,1,0:T(8,128)} %weight_hbm.1), custom_call_target="tpu_custom_call" | custom-call | tf_op jit(solution)/shard_map/pallas_call | solution.py:461

commit v6 on v2

--- a/solution.py
+++ b/solution.py
@@ -319,7 +319,7 @@
     per_date = offsets.shape[0]
     pairs = dates * per_date
     rows = phases.shape[0]
-    chunk = 4
+    chunk = (lines + 1) // 2
     fetches = [
         pltpu.make_async_copy(
             images_hbm.at[pl.ds(at, min(chunk, lines - at))],
@@ -403,7 +403,7 @@
     def backward(x):
         return mm(design2_t, jnp.concatenate(split(x), axis=0))
 
-    group = 8 if rows % 8 == 0 else 1
+    group = 16 if rows % 16 == 0 else 1
 
     def invert(at, carry):
         lanes = range(group)

time: 45.5 us -> 44.5 us (0.978)
  Pallas kernels: 45.4 us -> 44.3 us
    pallas_call x1, Pallas kernels: 34.8 us -> 33.8 us  [solve(): pl.pallas_call(functools.partial(solve_kernel, tiles), out_shape=jax.Shap...]
where the time goes in v6:
time: 44.5 us; the launch traced here: 44.3 us
  Pallas kernels  44.3 us (100%)
    pallas_call x1, Pallas kernels, solve(): pl.pallas_call(functools.partial(solve_kernel, tiles), out_shape=jax.Shap...  33.8 us
    pallas_call x1, Pallas kernels, exchange(): pl.pallas_call(functools.partial(exchange_kernel, tiles), out_shape=jax.S...  10.6 us

profile of v6, /device:TPU:19, one launch (start us, length us, event | category | flops | bytes accessed | tf_op | source)
XLA Modules:
  0.0 44.3 jit_solution(16761065440705304982)
XLA Ops:
  0.0 10.6 %shard_map.46.images_hbm = bf16[34,32,512]{2,1,0:T(8,128)(2,1)} custom-call(bf16[16,32,256]{2,1,0:T(8,128)(2,1)} %re_hbm.1, bf16[16,32,256]{2,1,0:T(8,128)(2,1)} %im_hbm.1), custom_call_target="tpu_custom_call" | custom-call | tf_op jit(solution)/shard_map/pallas_call | solution.py:196
  10.6 33.8 %shard_map.47 = f32[31,16,256]{2,1,0:T(8,128)} custom-call(bf16[34,32,512]{2,1,0:T(8,128)(2,1)} %shard_map.46.images_hbm, s32[4,32]{1,0:T(4,128)} %bitcast.1, s32[128,16,256]{2,1,0:T(8,128)} %weight_hbm.1), custom_call_target="tpu_custom_call" | custom-call | tf_op jit(solution)/shard_map/pallas_call | solution.py:455
